TPU v7x, 1024 devices: a whole 4x8x16 slice. The times are simulated.
1024 devices in a mesh: grp: 64 (over z, y_lo), mem: 16 (over y_hi, x, core).
Axes of the slice: x: 4, y: 8 (y_hi: 2, y_lo: 4; y = y_hi * 4 + y_lo), z: 16, core: 2. Of those that a mesh axis runs over, the one named last changes fastest.
Arguments:
- student: bfloat16 [196608, 512], P(('grp', 'mem')), may hold values from -6 to 6
- teacher: bfloat16 [196608, 1280], P(('grp', 'mem')), may hold values from -6 to 6
- block_target: float32 [196608, 3072], P(('grp', 'mem')), may hold values from -1 to 1
Outputs:
- student_grad: float32 [196608, 512], P(('grp', 'mem'))
All inputs are finite; a program needn't handle non-finite values.
Results may differ from a plain program's by a relative error of at most 0.0031.
Values may be sent and summed in bfloat16 or wider, within the bound.
A program may use at most 32 MiB of HBM per device.

v0:
```python
import math

import jax
import jax.numpy as jnp
from jax import lax
from jax.sharding import PartitionSpec as P

REACH = 3


def passed_along(block, axis, distance):
    devices = range(lax.axis_size(axis))
    route = [((i - distance) % len(devices), i) for i in devices]
    return lax.ppermute(block, axis, route)


def normalize(values):
    wide = values.astype(jnp.float32)
    return (wide * lax.rsqrt(jnp.sum(wide * wide, axis=1, keepdims=True) + 1e-06)).astype(
        jnp.bfloat16
    )


def body(student, teacher, block_target):
    own_count = student.shape[0]
    swidth = student.shape[1]
    weight = 16.0 * math.sqrt(swidth / (own_count * lax.axis_size("mem")))
    snorm = normalize(student)
    tnorm = normalize(teacher)
    contract = (((1,), (1,)), ((), ()))
    high = lax.Precision.HIGHEST
    block = lax.all_gather(snorm, "mem", axis=0, tiled=True)
    inner = (
        lax.dot_general(snorm, block, contract, preferred_element_type=jnp.float32) - block_target
    )
    grad = jnp.dot(inner, block.astype(jnp.float32), precision=high)
    own_feats = jnp.concatenate([snorm, tnorm], axis=1)

    def cross_of(travel):
        return lax.dot_general(
            snorm, travel[:, :swidth], contract, preferred_element_type=jnp.float32
        ) - lax.dot_general(tnorm, travel[:, swidth:], contract, preferred_element_type=jnp.float32)

    ahead = own_feats
    behind = own_feats
    for reach_step in range(REACH):
        ahead = passed_along(ahead, "grp", -1)
        cross = cross_of(ahead)
        grad = grad + jnp.dot(cross, ahead[:, :swidth].astype(jnp.float32), precision=high)
        behind = passed_along(behind, "grp", 1)
        cross = cross_of(behind)
        grad = grad + jnp.dot(cross, behind[:, :swidth].astype(jnp.float32), precision=high)
    return grad * weight


def solution(mesh):
    return jax.shard_map(
        body,
        mesh=mesh,
        in_specs=(P(("grp", "mem"), None), P(("grp", "mem"), None), P(("grp", "mem"), None)),
        out_specs=P(("grp", "mem"), None),
        check_vma=False,
    )
```

profile of v0, /device:TPU:1, one launch (start us, length us, event | category | flops | bytes accessed | tf_op | source)
XLA Modules:
  0.0 173.5 jit_solution(416834647972781370)
XLA Ops:
  6.5 0.0 all-gather.2.cloned.1.call-start
  6.5 1.0 fusion.17
  7.6 1.7 fusion.18
  9.3 0.0 all-gather.2.cloned.1.call-update
  9.3 1.3 fusion.3
  10.6 1.2 fusion.4
  11.8 1.0 pad_maximum_fusion
  12.8 21.8 %collective-permute-start = (bf16[192,1792]{1,0:T(8,128)(2,1)S(1)}, bf16[192,1792]{1,0:T(8,128)(2,1)S(1)}, u32[]{:S(2)}, u32[]{:S(2)}) collective-permute-start(bf16[192,1792]{1,0:T(8,128)(2,1)S(1)} %pad_maximum_fusion), channel_id=1, source_target_pairs={{16,0},{32,16},{48,32},{64,48},{80,64},{96,80},{112,96},{128,112},... | collective-permute-start | bytes 2064392 | tf_op jit(solution)/shard_map/ppermute | solution.py:14
  34.6 1.9 %collective-permute-start.1 = (bf16[192,1792]{1,0:T(8,128)(2,1)S(1)}, bf16[192,1792]{1,0:T(8,128)(2,1)S(1)}, u32[]{:S(2)}, u32[]{:S(2)}) collective-permute-start(bf16[192,1792]{1,0:T(8,128)(2,1)S(1)} %pad_maximum_fusion), channel_id=1, source_target_pairs={{1008,0},{0,16},{16,32},{32,48},{48,64},{64,80},{80,96},{96,112},{... | collective-permute-start | bytes 2064392 | tf_op jit(solution)/shard_map/ppermute | solution.py:14
  36.5 12.2 %collective-permute-done = bf16[192,1792]{1,0:T(8,128)(2,1)S(1)} collective-permute-done((bf16[192,1792]{1,0:T(8,128)(2,1)S(1)}, bf16[192,1792]{1,0:T(8,128)(2,1)S(1)}, u32[]{:S(2)}, u32[]{:S(2)}) %collective-permute-start) | collective-permute-done | bytes 688160 | tf_op jit(solution)/shard_map/ppermute | solution.py:14
  48.7 21.0 %collective-permute-start.2 = (bf16[192,1792]{1,0:T(8,128)(2,1)S(1)}, bf16[192,1792]{1,0:T(8,128)(2,1)S(1)}, u32[]{:S(2)}, u32[]{:S(2)}) collective-permute-start(bf16[192,1792]{1,0:T(8,128)(2,1)S(1)} %collective-permute-done), channel_id=1, source_target_pairs={{16,0},{32,16},{48,32},{64,48},{80,64},{96,80},{112,96},{128,112},... | collective-permute-start | bytes 2064392 | tf_op jit(solution)/shard_map/ppermute | solution.py:14
  69.7 0.0 collective-permute-done.1
  69.7 1.9 %collective-permute-start.3 = (bf16[192,1792]{1,0:T(8,128)(2,1)S(1)}, bf16[192,1792]{1,0:T(8,128)(2,1)S(1)}, u32[]{:S(2)}, u32[]{:S(2)}) collective-permute-start(bf16[192,1792]{1,0:T(8,128)(2,1)S(1)} %collective-permute-done.1), channel_id=1, source_target_pairs={{1008,0},{0,16},{16,32},{32,48},{48,64},{64,80},{80,96},{96,112},{... | collective-permute-start | bytes 2064392 | tf_op jit(solution)/shard_map/ppermute | solution.py:14
  71.6 0.3 fusion.15
  72.0 0.9 convolution_subtract_fusion.6
  72.9 0.3 fusion.13
  73.2 0.2 convolution_subtract_fusion.5
  73.4 9.5 %collective-permute-done.2 = bf16[192,1792]{1,0:T(8,128)(2,1)S(1)} collective-permute-done((bf16[192,1792]{1,0:T(8,128)(2,1)S(1)}, bf16[192,1792]{1,0:T(8,128)(2,1)S(1)}, u32[]{:S(2)}, u32[]{:S(2)}) %collective-permute-start.2) | collective-permute-done | bytes 688160 | tf_op jit(solution)/shard_map/ppermute | solution.py:14
  82.9 32.3 %collective-permute-start.4 = (bf16[192,1792]{1,0:T(8,128)(2,1)S(1)}, bf16[192,1792]{1,0:T(8,128)(2,1)S(1)}, u32[]{:S(2)}, u32[]{:S(2)}) collective-permute-start(bf16[192,1792]{1,0:T(8,128)(2,1)S(1)} %collective-permute-done.2), channel_id=1, source_target_pairs={{16,0},{32,16},{48,32},{64,48},{80,64},{96,80},{112,96},{128,112},... | collective-permute-start | bytes 2064392 | tf_op jit(solution)/shard_map/ppermute | solution.py:14
  115.2 0.0 collective-permute-done.3
  115.2 1.9 %collective-permute-start.5 = (bf16[192,1792]{1,0:T(8,128)(2,1)S(1)}, bf16[192,1792]{1,0:T(8,128)(2,1)S(1)}, u32[]{:S(2)}, u32[]{:S(2)}) collective-permute-start(bf16[192,1792]{1,0:T(8,128)(2,1)S(1)} %collective-permute-done.3), channel_id=1, source_target_pairs={{1008,0},{0,16},{16,32},{32,48},{48,64},{64,80},{80,96},{96,112},{... | collective-permute-start | bytes 2064392 | tf_op jit(solution)/shard_map/ppermute | solution.py:14
  117.1 0.3 fusion.11
  117.4 0.3 fusion.9
  117.8 0.9 convolution_subtract_fusion.4
  118.7 0.2 convolution_subtract_fusion.3
  118.9 0.3 fusion.24
  119.2 0.0 copy-done.8
  119.2 0.0 copy-start.2
  119.3 6.0 %collective-permute-done.4 = bf16[192,1792]{1,0:T(8,128)(2,1)S(1)} collective-permute-done((bf16[192,1792]{1,0:T(8,128)(2,1)S(1)}, bf16[192,1792]{1,0:T(8,128)(2,1)S(1)}, u32[]{:S(2)}, u32[]{:S(2)}) %collective-permute-start.4) | collective-permute-done | bytes 688160 | tf_op jit(solution)/shard_map/ppermute | solution.py:14
  125.2 0.3 fusion.7
  125.6 0.9 convolution_subtract_fusion.2
  126.5 28.0 %collective-permute-done.5 = bf16[192,1792]{1,0:T(8,128)(2,1)S(1)} collective-permute-done((bf16[192,1792]{1,0:T(8,128)(2,1)S(1)}, bf16[192,1792]{1,0:T(8,128)(2,1)S(1)}, u32[]{:S(2)}, u32[]{:S(2)}) %collective-permute-start.5) | collective-permute-done | bytes 688160 | tf_op jit(solution)/shard_map/ppermute | solution.py:14
  154.5 0.3 fusion.5
  154.8 0.0 copy-done.9
  154.8 0.2 convolution_subtract_fusion.1
  155.0 0.3 fusion.19
  155.4 0.0 all-gather.2.cloned.1.call-done
  155.4 3.2 %convolution_subtract_fusion = f32[192,3072]{1,0:T(8,128)S(1)} fusion(f32[192,3072]{1,0:T(8,128)S(1)} %copy-done.2, bf16[192,512]{1,0:T(8,128)(2,1)S(1)} %copy-done, bf16[3072,512]{1,0:T(8,128)(2,1)} %all-gather.2.cloned.1.call-done), kind=kOutput, calls=%fused_computation | convolution fusion | flops 604569600 | bytes 8060928 | tf_op jit(solution)/shard_map/dot_general | solution.py:34
  158.6 0.0 copy-done.1
  158.6 0.0 copy-start.3
  158.6 2.0 %fusion.33 = f32[192,512]{1,0:T(8,128)S(1)} fusion(f32[192,3072]{1,0:T(8,128)S(1)} %convolution_subtract_fusion, bf16[3072,512]{1,0:T(8,128)(2,1)S(1)} %copy-done.1), kind=kOutput, calls=%fused_computation.51 | convolution fusion | flops 3623878656 | bytes 5898240 | tf_op jit(solution)/shard_map/dot_general | solution.py:36
  160.7 0.0 copy-done.3
  160.7 0.0 copy-start.4
  160.7 0.0 copy-start.5
  160.7 1.3 convolution_add_fusion.3
  162.0 1.3 convolution_add_fusion.2
  163.3 1.3 fusion
  164.6 2.0 %fusion.2 = f32[192,512]{1,0:T(8,128)} fusion(f32[192,512]{1,0:T(8,128)S(1)} %fusion.19, f32[192,512]{1,0:T(8,128)S(1)} %fusion, f32[192,192]{1,0:T(8,128)S(1)} %copy-done.5, bf16[192,1792]{1,0:T(8,128)(2,1)} %copy-done.9), kind=kOutput, calls=%fused_computation.9 | convolution fusion | flops 226787328 | bytes 1523712 | tf_op jit(solution)/shard_map/dot_general | solution.py:49
  (14 shorter events, 0.0 us)
Async XLA Ops:
  6.5 148.8 %all-gather.2.cloned.1.call-start = ((), (), s32[]{:S(2)}) async-start(), calls=%async_computation | async-start | bytes 3342336 | tf_op jit(solution)/shard_map/all_gather | solution.py:32
  9.3 62.7 %copy-start = (bf16[192,512]{1,0:T(8,128)(2,1)S(1)}, bf16[192,512]{1,0:T(8,128)(2,1)}, u32[]{:S(2)}) copy-start(bf16[192,512]{1,0:T(8,128)(2,1)} %fusion.18) | copy-start | bytes 589828
  12.8 35.9 %collective-permute-start = (bf16[192,1792]{1,0:T(8,128)(2,1)S(1)}, bf16[192,1792]{1,0:T(8,128)(2,1)S(1)}, u32[]{:S(2)}, u32[]{:S(2)}) collective-permute-start(bf16[192,1792]{1,0:T(8,128)(2,1)S(1)} %pad_maximum_fusion), channel_id=1, source_target_pairs={{16,0},{32,16},{48,32},{64,48},{80,64},{96,80},{112,96},{128,112},... | collective-permute-start | bytes 2064392 | tf_op jit(solution)/shard_map/ppermute | solution.py:14
  34.6 35.1 %collective-permute-start.1 = (bf16[192,1792]{1,0:T(8,128)(2,1)S(1)}, bf16[192,1792]{1,0:T(8,128)(2,1)S(1)}, u32[]{:S(2)}, u32[]{:S(2)}) collective-permute-start(bf16[192,1792]{1,0:T(8,128)(2,1)S(1)} %pad_maximum_fusion), channel_id=1, source_target_pairs={{1008,0},{0,16},{16,32},{32,48},{48,64},{64,80},{80,96},{96,112},{... | collective-permute-start | bytes 2064392 | tf_op jit(solution)/shard_map/ppermute | solution.py:14
  48.7 68.7 %copy-start.6 = (bf16[192,1792]{1,0:T(8,128)(2,1)}, bf16[192,1792]{1,0:T(8,128)(2,1)S(1)}, u32[]{:S(2)}) copy-start(bf16[192,1792]{1,0:T(8,128)(2,1)S(1)} %collective-permute-done) | copy-start | bytes 2064388
  48.7 34.2 %collective-permute-start.2 = (bf16[192,1792]{1,0:T(8,128)(2,1)S(1)}, bf16[192,1792]{1,0:T(8,128)(2,1)S(1)}, u32[]{:S(2)}, u32[]{:S(2)}) collective-permute-start(bf16[192,1792]{1,0:T(8,128)(2,1)S(1)} %collective-permute-done), channel_id=1, source_target_pairs={{16,0},{32,16},{48,32},{64,48},{80,64},{96,80},{112,96},{128,112},... | collective-permute-start | bytes 2064392 | tf_op jit(solution)/shard_map/ppermute | solution.py:14
  69.7 47.7 %copy-start.7 = (bf16[192,1792]{1,0:T(8,128)(2,1)}, bf16[192,1792]{1,0:T(8,128)(2,1)S(1)}, u32[]{:S(2)}) copy-start(bf16[192,1792]{1,0:T(8,128)(2,1)S(1)} %collective-permute-done.1) | copy-start | bytes 2064388
  69.7 45.5 %collective-permute-start.3 = (bf16[192,1792]{1,0:T(8,128)(2,1)S(1)}, bf16[192,1792]{1,0:T(8,128)(2,1)S(1)}, u32[]{:S(2)}, u32[]{:S(2)}) collective-permute-start(bf16[192,1792]{1,0:T(8,128)(2,1)S(1)} %collective-permute-done.1), channel_id=1, source_target_pairs={{1008,0},{0,16},{16,32},{32,48},{48,64},{64,80},{80,96},{96,112},{... | collective-permute-start | bytes 2064392 | tf_op jit(solution)/shard_map/ppermute | solution.py:14
  82.9 36.3 %copy-start.8 = (bf16[192,1792]{1,0:T(8,128)(2,1)}, bf16[192,1792]{1,0:T(8,128)(2,1)S(1)}, u32[]{:S(2)}) copy-start(bf16[192,1792]{1,0:T(8,128)(2,1)S(1)} %collective-permute-done.2) | copy-start | bytes 2064388
  82.9 42.3 %collective-permute-start.4 = (bf16[192,1792]{1,0:T(8,128)(2,1)S(1)}, bf16[192,1792]{1,0:T(8,128)(2,1)S(1)}, u32[]{:S(2)}, u32[]{:S(2)}) collective-permute-start(bf16[192,1792]{1,0:T(8,128)(2,1)S(1)} %collective-permute-done.2), channel_id=1, source_target_pairs={{16,0},{32,16},{48,32},{64,48},{80,64},{96,80},{112,96},{128,112},... | collective-permute-start | bytes 2064392 | tf_op jit(solution)/shard_map/ppermute | solution.py:14
  115.2 39.3 %collective-permute-start.5 = (bf16[192,1792]{1,0:T(8,128)(2,1)S(1)}, bf16[192,1792]{1,0:T(8,128)(2,1)S(1)}, u32[]{:S(2)}, u32[]{:S(2)}) collective-permute-start(bf16[192,1792]{1,0:T(8,128)(2,1)S(1)} %collective-permute-done.3), channel_id=1, source_target_pairs={{1008,0},{0,16},{16,32},{32,48},{48,64},{64,80},{80,96},{96,112},{... | collective-permute-start | bytes 2064392 | tf_op jit(solution)/shard_map/ppermute | solution.py:14
  119.2 36.1 %copy-start.2 = (f32[192,3072]{1,0:T(8,128)S(1)}, f32[192,3072]{1,0:T(8,128)}, u32[]{:S(2)}) copy-start(f32[192,3072]{1,0:T(8,128)} %param.5) | copy-start | bytes 7077892
  125.2 29.5 %copy-start.9 = (bf16[192,1792]{1,0:T(8,128)(2,1)}, bf16[192,1792]{1,0:T(8,128)(2,1)S(1)}, u32[]{:S(2)}) copy-start(bf16[192,1792]{1,0:T(8,128)(2,1)S(1)} %collective-permute-done.4) | copy-start | bytes 2064388
  155.4 3.2 %copy-start.1 = (bf16[3072,512]{1,0:T(8,128)(2,1)S(1)}, bf16[3072,512]{1,0:T(8,128)(2,1)}, u32[]{:S(2)}) copy-start(bf16[3072,512]{1,0:T(8,128)(2,1)} %all-gather.2.cloned.1.call-done) | copy-start | bytes 9437188
  158.6 2.1 %copy-start.3 = (f32[192,192]{1,0:T(8,128)S(1)}, f32[192,192]{1,0:T(8,128)}, u32[]{:S(2)}) copy-start(f32[192,192]{1,0:T(8,128)} %convolution_subtract_fusion.6) | copy-start | bytes 442372
  160.7 2.6 %copy-start.4 = (f32[192,192]{1,0:T(8,128)S(1)}, f32[192,192]{1,0:T(8,128)}, u32[]{:S(2)}) copy-start(f32[192,192]{1,0:T(8,128)} %convolution_subtract_fusion.4) | copy-start | bytes 442372
  160.7 3.9 %copy-start.5 = (f32[192,192]{1,0:T(8,128)S(1)}, f32[192,192]{1,0:T(8,128)}, u32[]{:S(2)}) copy-start(f32[192,192]{1,0:T(8,128)} %convolution_subtract_fusion.2) | copy-start | bytes 442372
Sparse Core Ops, SparseCore 0:
  11.8 118.6 all-gather.1
where the time goes:
time: 174 us; the launch traced here: 173 us
  starting transfers between devices  80.8 us (46%)
  waiting for transfers between devices  55.7 us (32%)
  matrix products  17 us (10%)
  between operations  13.7 us (8%)
  other arithmetic  6.18 us (4%)
    ppermute x6, starting transfers between devices, passed_along(): return lax.ppermute(block, axis, route)  80.8 us
    ppermute x6, waiting for transfers between devices, passed_along(): return lax.ppermute(block, axis, route)  55.6 us
    dot_general x3, matrix products, body(): jnp.dot(cross, ahead[:, :swidth].astype(jnp.float32), precision=high)  4.61 us
  transfers between devices with their start and end apart: 7, of which 4 were waited for; matrix products, arithmetic and copies ran while one was open for 5% of the time, Pallas kernels for 0%

commit v1 on v0

v1 whole, which is shorter than its diff:
```python
import math

import jax
import jax.numpy as jnp
from jax import lax
from jax.experimental import pallas as pl
from jax.experimental.pallas import tpu as pltpu
from jax.sharding import PartitionSpec as P

MESH = pl.DeviceIdType.MESH
NX, NY, NZ, LINE = 4, 8, 16, 4
F32, BF16 = jnp.float32, jnp.bfloat16

CHAIN, XO, XQ, SIB = 0, 4, 7, 10
TLINE, SRIGHT = 18, 22
ZS, ZT, WS, WT, PZ, PF = 23, 27, 31, 32, 33, 37
COPIES = 41
RIGHT, LEFT, TWO, ZUP, ZDOWN, XUP, XDOWN, XTWO, CORE = range(9)
BACK = (LEFT, RIGHT, TWO, ZDOWN, ZUP, XDOWN, XUP, XTWO, CORE)
HOPS = (1, 3, 2)


def dot_t(a, b):
    return lax.dot_general(a, b, (((1,), (1,)), ((), ())), preferred_element_type=F32)


def t_dot(a, b):
    return lax.dot_general(a, b, (((0,), (0,)), ((), ())), preferred_element_type=F32)


def normalize(values):
    wide = values.astype(F32)
    return (wide * lax.rsqrt(jnp.sum(wide * wide, axis=1, keepdims=True) + 1e-06)).astype(BF16)


def kernel(
    student, teacher, target, out,
    blk, sp, tp, sq, tq, pin, pz, pzo, po, pacc, tgt, acc, ready, ssem, rsem, lsem,
):
    grp, mem = lax.axis_index("grp"), lax.axis_index("mem")
    z, a = grp // LINE, grp % LINE
    r, x, c = mem // 8, (mem // 2) % NX, mem % 2
    y = r * LINE + a
    way = 1 - 2 * c
    p = a + c * (3 - 2 * a)
    a_meet = 2 - c
    a_of = lambda place: place + c * (3 - 2 * place)
    meet = p == 2
    first_z, last_z = z == 0, z == NZ - 1
    rows = sp.shape[1]

    def at(dz=0, dy=0, dx=0, dc=0):
        yy, zz, xx = (y + dy + NY) % NY, (z + dz + NZ) % NZ, (x + dx) % NX
        cc = (c + dc) % 2
        rank = ((zz * NY + yy) * NX + xx) * 2 + cc
        rank = jnp.where(rank == 0, 2 * NX * NY * NZ, rank)
        return (zz * LINE + yy % LINE, (yy // LINE) * 8 + xx * 2 + cc), rank

    _, my_rank = at()
    two = jnp.where(p == 0, 2, -2) * way
    near = [at(dy=way), at(dy=-way), at(dy=two), at(dz=1), at(dz=-1), at(dx=1), at(dx=3), at(dx=2), at(dc=1)]
    used = [None, None, (p == 0) | (p == 2)] + [None] * 6
    earlier = [rank < my_rank for _, rank in near]
    dev = [d for d, _ in near]

    def over(n, cond):
        return cond if used[n] is None else cond & used[n]

    barrier = pltpu.get_barrier_semaphore()
    for n in range(9):
        @pl.when(over(n, jnp.logical_not(earlier[n])))
        def _():
            pl.semaphore_signal(barrier, 1, device_id=dev[n], device_id_type=MESH)

    load = pltpu.make_async_copy(target, tgt, lsem)
    load.start()
    me = r * 8 + x * 2 + c
    partner = (1 - r) * 8 + x * 2 + c
    own = normalize(student[...])
    sp[a] = own
    blk[me] = own
    tp[a] = normalize(teacher[...])

    peers = sum(over(n, earlier[n]).astype(jnp.int32) for n in range(9))
    @pl.when(peers > 0)
    def _():
        pl.semaphore_wait(barrier, peers)

    for n in range(9):
        @pl.when(over(n, earlier[n]))
        def _():
            pl.semaphore_signal(ready.at[BACK[n]], 1, device_id=dev[n], device_id_type=MESH)

    def wait_ready(n, cond=None):
        here = jnp.logical_not(earlier[n])
        here = over(n, here if cond is None else here & cond)
        @pl.when(here)
        def _():
            pl.semaphore_wait(ready.at[n], 1)

    started = []

    def send(i, src, dst, n, cond=None):
        copy = pltpu.make_async_remote_copy(
            src_ref=src, dst_ref=dst, send_sem=ssem.at[i], recv_sem=rsem.at[i],
            device_id=dev[n], device_id_type=MESH,
        )
        started.append((copy, cond))
        if cond is None:
            copy.start()
        else:
            pl.when(cond)(copy.start)

    def recv(i, dst, cond=None):
        copy = pltpu.make_async_remote_copy(
            src_ref=dst, dst_ref=dst, send_sem=ssem.at[i], recv_sem=rsem.at[i],
            device_id=dev[RIGHT], device_id_type=MESH,
        )
        if cond is None:
            copy.wait_recv()
        else:
            pl.when(cond)(copy.wait_recv)

    def chain_slot(d):
        yo = (y - d * way + NY) % NY
        return yo % LINE, (yo // LINE) * 8 + x * 2 + c

    def chain_send(d):
        ao, mo = chain_slot(d)
        src = sp.at[4] if d == 3 else sp.at[ao]
        dst = sp.at[ao] if d < 2 else sp.at[4] if d == 2 else blk.at[mo]
        send(CHAIN + d, src, dst, RIGHT)

    def chain_recv(d):
        ao, mo = chain_slot(d)
        recv(CHAIN + d - 1, sp.at[ao] if d < 3 else sp.at[4] if d == 3 else blk.at[mo])

    def x_send(base, whose):
        for k, n in enumerate((XUP, XDOWN, XTWO)):
            send(base + k, blk.at[whose], blk.at[whose], n)

    def sib_send(i, whose):
        send(SIB + i, blk.at[whose], blk.at[whose], CORE)

    def x_recv(base, part, sib):
        for k in range(3):
            whose = part * 8 + ((x + NX - HOPS[k]) % NX) * 2 + c
            recv(base + k, blk.at[whose])
            sib_send(sib + 1 + k, whose)

    def sib_recv(part, sib):
        for k in range(4):
            xx = x if k == 0 else (x + NX - HOPS[k - 1]) % NX
            recv(SIB + sib + k, blk.at[part * 8 + xx * 2 + 1 - c])

    def inner(part):
        def step(k, _):
            chip = part * 4 + k
            pair = jnp.concatenate([blk[2 * chip], blk[2 * chip + 1]], axis=0)
            cols = pl.ds(pl.multiple_of(chip * 2 * rows, 128), 2 * rows)
            affinity = dot_t(sp[a], pair) - tgt[:, cols]
            acc[...] += jnp.dot(affinity.astype(BF16), pair, preferred_element_type=F32)
            return 0

        lax.fori_loop(0, 4, step, 0)

    wait_ready(LEFT, p == 3)
    send(SRIGHT, sp.at[a], sp.at[a], LEFT, p == 3)
    send(TLINE + 3, tp.at[a], tp.at[a], LEFT, p == 3)
    wait_ready(RIGHT)
    chain_send(0)
    send(TLINE + 1, tp.at[a], tp.at[a], RIGHT, p == 1)
    wait_ready(TWO, p == 0)
    send(TLINE + 0, tp.at[a], tp.at[a], TWO, p == 0)
    wrap_out = last_z & jnp.logical_not(meet) & (a > 0)
    wrap_in = first_z & jnp.logical_not(meet) & (a > 0)
    up_now = meet | wrap_out
    forward = meet & jnp.logical_not(last_z)
    wait_ready(ZUP, up_now)
    send(ZS, sp.at[a], sq.at[a], ZUP, meet)
    send(ZT, tp.at[a], tq.at[a], ZUP, meet)
    send(WS, sp.at[a], sq.at[a], ZUP, wrap_out)
    send(WT, tp.at[a], tq.at[a], ZUP, wrap_out)
    wait_ready(CORE)
    sib_send(0, me)
    for n in (XUP, XDOWN, XTWO):
        wait_ready(n)
    x_send(XO, me)

    a_next, a_last = 3 - a_meet, 3
    chain_recv(1)
    chain_send(1)
    send(ZS + 1, sp.at[a_next], sq.at[a_next], ZUP, forward)
    chain_recv(2)
    chain_send(2)
    send(ZS + 2, sp.at[a_last], sq.at[a_last], ZUP, forward & (c == 1))
    recv(TLINE + 1, tp.at[a_next], meet)
    send(ZT + 1, tp.at[a_next], tq.at[a_next], ZUP, forward)
    x_recv(XO, r, 0)
    chain_recv(3)
    chain_send(3)
    recv(SRIGHT, sp.at[a_of(3)], meet)
    send(ZS + 2, sp.at[a_last], sq.at[a_last], ZUP, forward & (c == 0))
    recv(TLINE + 3, tp.at[a_of(3)], meet)
    send(ZT + 2, tp.at[a_last], tq.at[a_last], ZUP, forward & (c == 0))
    recv(TLINE + 0, tp.at[a_of(0)], meet)
    send(ZT + 2, tp.at[a_last], tq.at[a_last], ZUP, forward & (c == 1))

    @pl.when(meet)
    def _():
        pacc[...] = jnp.zeros_like(pacc)

        def outer(j, _):
            def step(i, _):
                cross = (dot_t(sp[i], sp[j]) - dot_t(tp[i], tp[j])).astype(BF16)
                pacc[i] += jnp.dot(cross, sp[j], preferred_element_type=F32)
                pacc[j] += t_dot(cross, sp[i])
                return 0

            return lax.fori_loop(0, j, step, 0)

        lax.fori_loop(1, LINE, outer, 0)

    chain_recv(4)
    sib_send(4, partner)
    x_send(XQ, partner)

    def across(i):
        acc[...] = jnp.zeros_like(acc)

        def step(j, _):
            cross = (dot_t(sq[i], sp[j]) - dot_t(tq[i], tp[j])).astype(BF16)
            acc[...] += jnp.dot(cross, sp[j], preferred_element_type=F32)
            pacc[j] += t_dot(cross, sq[i])
            return 0

        lax.fori_loop(0, i, step, 0)
        pzo[i] = acc[...].astype(BF16)

    def across_at(k, i):
        recv(ZS + k, sq.at[i], meet)
        recv(ZT + k, tq.at[i], meet)
        pl.when(meet)(lambda: across(i))
        send(PZ + k, pzo.at[i], pz.at[i], ZDOWN, meet)

    wait_ready(ZDOWN, meet)
    across_at(0, a_meet)
    across_at(1, a_next)

    recv(WS, sq.at[a], wrap_in)
    recv(WT, tq.at[a], wrap_in)
    seam_left = wrap_in & (p == 3)
    seam_right = wrap_in & (p == 1)
    seam_two = wrap_in & (p == 0)
    for i, buf in ((ZS, sq), (ZT, tq)):
        send(i + 2, buf.at[a], buf.at[a], LEFT, seam_left)
        send(i + 1, buf.at[a], buf.at[a], RIGHT, seam_right)
        send(i + 2, buf.at[a], buf.at[a], TWO, seam_two)

    x_recv(XQ, 1 - r, 4)
    across_at(2, a_last)

    wait_ready(LEFT, meet)
    wait_ready(TWO, meet)
    for k, i in enumerate((a_meet, a_next, a_last)):
        recv(PZ + k, pz.at[i], meet)

    @pl.when(meet)
    def _():
        for i in range(1, LINE):
            pacc[i] += pz[i].astype(F32)
        po[...] = pacc[...].astype(BF16)

    for place, n in ((0, TWO), (1, LEFT), (3, RIGHT)):
        send(PF + place, po.at[a_of(place)], pin, n, meet)

    acc[...] = jnp.zeros_like(acc)
    load.wait()
    sib_recv(r, 0)
    inner(r)
    sib_recv(1 - r, 4)
    inner(1 - r)

    @pl.when(meet)
    def _():
        out[...] = acc[...] + pacc[a]

    for place in (0, 1, 3):
        recv(PF + place, pin, p == place)

    @pl.when(jnp.logical_not(meet))
    def _():
        out[...] = acc[...] + pin[...].astype(F32)

    wait_ready(LEFT, (p == 0) | (p == 1))
    wait_ready(ZUP, jnp.logical_not(up_now))
    wait_ready(ZDOWN, jnp.logical_not(meet))
    for copy, cond in started:
        if cond is None:
            copy.wait_send()
        else:
            pl.when(cond)(copy.wait_send)


def body(student, teacher, block_target):
    rows, ds = student.shape
    dt = teacher.shape[1]
    columns = block_target.shape[1]
    weight = 16.0 * math.sqrt(ds / columns)
    vmem = pl.BlockSpec(memory_space=pltpu.VMEM)
    part = pl.pallas_call(
        kernel,
        out_shape=jax.ShapeDtypeStruct((rows, ds), F32),
        in_specs=[vmem, vmem, pl.BlockSpec(memory_space=pl.ANY)],
        out_specs=vmem,
        scratch_shapes=[
            pltpu.VMEM((16, rows, ds), BF16),
            pltpu.VMEM((5, rows, ds), BF16),
            pltpu.VMEM((4, rows, dt), BF16),
            pltpu.VMEM((4, rows, ds), BF16),
            pltpu.VMEM((4, rows, dt), BF16),
            pltpu.VMEM((rows, ds), BF16),
            pltpu.VMEM((4, rows, ds), BF16),
            pltpu.VMEM((4, rows, ds), BF16),
            pltpu.VMEM((4, rows, ds), BF16),
            pltpu.VMEM((4, rows, ds), F32),
            pltpu.VMEM((rows, columns), F32),
            pltpu.VMEM((rows, ds), F32),
            pltpu.SemaphoreType.REGULAR((9,)),
            pltpu.SemaphoreType.DMA((COPIES,)),
            pltpu.SemaphoreType.DMA((COPIES,)),
            pltpu.SemaphoreType.DMA,
        ],
        compiler_params=pltpu.CompilerParams(
            collective_id=0, has_side_effects=True, vmem_limit_bytes=48 * 2**20
        ),
    )(student, teacher, block_target)
    return part * weight


def solution(mesh):
    spec = P(("grp", "mem"), None)
    return jax.shard_map(body, mesh=mesh, in_specs=(spec,) * 3, out_specs=spec, check_vma=False)
```

time: 174 us -> 65 us (0.37)
  starting transfers between devices: 80.8 us -> 0 us
  Pallas kernels: 0 us -> 60.2 us
  waiting for transfers between devices: 55.7 us -> 0 us
  matrix products: 17 us -> 0 us
  between operations: 13.7 us -> 0.01 us
  other arithmetic: 6.18 us -> 0.78 us
  local copies, waits for them, and re-layouts: 0.04 us -> 3.62 us
    ppermute x6 -> x0, starting transfers between devices: 80.8 us -> none  [passed_along(): return lax.ppermute(block, axis, route)]
    pallas_call x0 -> x1, Pallas kernels: none -> 60.2 us  [body(): pl.pallas_call(kernel, out_shape=jax.ShapeDtypeStruct((rows, ds), F32), i...]
    ppermute x6 -> x0, waiting for transfers between devices: 55.6 us -> none  [passed_along(): return lax.ppermute(block, axis, route)]
    dot_general x20 -> x0, matrix products: 17 us -> none  [the longest x3 4.61 us: body(): jnp.dot(cross, ahead[:, :swidth].astype(jnp.float32), precision=high)]
    unnamed x20 -> x6, local copies, waits for them, and re-layouts: 0.04 us -> 3.62 us
    convert_element_type x2 -> x0, other arithmetic: 2.89 us -> none  [normalize(): (wide * lax.rsqrt(jnp.sum(wide * wide, axis=1, keepdims=True) + 1e-06)).a...]
    reduce_sum x2 -> x0, other arithmetic: 2.3 us -> none  [normalize(): jnp.sum(wide * wide, axis=1, keepdims=True) + 1e-06]
  transfers between devices with their start and end apart: 7 -> 0, of which waited for: 4 -> 0; matrix products, arithmetic and copies ran while one was open for 5% -> 0% of each run, Pallas kernels for 0% -> 0%
where the time goes in v1:
time: 65 us; the launch traced here: 64.7 us
  Pallas kernels  60.2 us (93%)
  local copies, waits for them, and re-layouts  3.62 us (6%)
  other arithmetic  0.78 us (1%)
    pallas_call x1, Pallas kernels, body(): pl.pallas_call(kernel, out_shape=jax.ShapeDtypeStruct((rows, ds), F32), i...  60.2 us
    unnamed x6, local copies, waits for them, and re-layouts  3.62 us

profile of v1, /device:TPU:1, one launch (start us, length us, event | category | flops | bytes accessed | tf_op | source)
XLA Modules:
  0.0 64.7 jit_solution(9410261276317927467)
XLA Ops:
  0.0 0.0 copy-start
  0.0 1.7 %copy-done = f32[192,3072]{1,0:T(8,128)S(1)} copy-done((f32[192,3072]{1,0:T(8,128)S(1)}, f32[192,3072]{1,0:T(8,128)}, u32[]{:S(2)}) %copy-start) | copy-done | bytes 2359320
  1.7 0.0 copy-start.1
  1.7 1.0 %copy-done.1 = bf16[192,1280]{1,0:T(8,128)(2,1)S(1)} copy-done((bf16[192,1280]{1,0:T(8,128)(2,1)S(1)}, bf16[192,1280]{1,0:T(8,128)(2,1)}, u32[]{:S(2)}) %copy-start.1) | copy-done | bytes 491544
  2.7 0.0 copy-start.2
  2.7 0.9 %copy-done.2 = bf16[192,512]{1,0:T(8,128)(2,1)S(1)} copy-done((bf16[192,512]{1,0:T(8,128)(2,1)S(1)}, bf16[192,512]{1,0:T(8,128)(2,1)}, u32[]{:S(2)}) %copy-start.2) | copy-done | bytes 196632
  3.6 60.2 %shard_map.37 = f32[192,512]{1,0:T(8,128)S(1)} custom-call(bf16[192,512]{1,0:T(8,128)(2,1)S(1)} %copy-done.2, bf16[192,1280]{1,0:T(8,128)(2,1)S(1)} %copy-done.1, f32[192,3072]{1,0:T(8,128)S(1)} %copy-done), custom_call_target="tpu_custom_call" | custom-call | tf_op jit(solution)/shard_map/pallas_call | solution.py:311
  63.9 0.8 %broadcast_multiply_fusion = f32[192,512]{1,0:T(8,128)} fusion(f32[192,512]{1,0:T(8,128)S(1)} %shard_map.37), kind=kLoop, calls=%fused_computation | loop fusion | flops 98304 | bytes 786432 | tf_op jit(solution)/shard_map/mul | solution.py:338
Async XLA Ops:
  0.0 1.7 %copy-start = (f32[192,3072]{1,0:T(8,128)S(1)}, f32[192,3072]{1,0:T(8,128)}, u32[]{:S(2)}) copy-start(f32[192,3072]{1,0:T(8,128)} %target.1) | copy-start | bytes 7077892
  1.7 1.0 %copy-start.1 = (bf16[192,1280]{1,0:T(8,128)(2,1)S(1)}, bf16[192,1280]{1,0:T(8,128)(2,1)}, u32[]{:S(2)}) copy-start(bf16[192,1280]{1,0:T(8,128)(2,1)} %teacher.1) | copy-start | bytes 1474564
  2.7 0.9 %copy-start.2 = (bf16[192,512]{1,0:T(8,128)(2,1)S(1)}, bf16[192,512]{1,0:T(8,128)(2,1)}, u32[]{:S(2)}) copy-start(bf16[192,512]{1,0:T(8,128)(2,1)} %student.1) | copy-start | bytes 589828

commit v2 on v1

v2 whole, which is shorter than its diff:
```python
import math

import jax
import jax.numpy as jnp
from jax import lax
from jax.experimental import pallas as pl
from jax.experimental.pallas import tpu as pltpu
from jax.sharding import PartitionSpec as P

MESH = pl.DeviceIdType.MESH
NX, NY, NZ, LINE = 4, 8, 16, 4
F32, BF16 = jnp.float32, jnp.bfloat16

XO, XQ, FAR, SIB, SIBQ = 0, 3, 9, 11, 15
SLINE, TLINE = 23, 27
ZS, ZT, WS, WT, RT, PZ, PF = 31, 34, 37, 38, 42, 46, 49
COPIES = 53
RIGHT, LEFT, TWO, HALF, ZUP, ZDOWN, XUP, XDOWN, XTWO, CORE, DNEXT, DLAST, UPMEET = range(13)
BACK = (LEFT, RIGHT, TWO, HALF, ZDOWN, ZUP, XDOWN, XUP, XTWO, CORE, UPMEET, UPMEET, None)
HOPS = (1, 3, 2)
PIECES = 4
PARTS = 2


def dot_t(a, b):
    return lax.dot_general(a, b, (((1,), (1,)), ((), ())), preferred_element_type=F32)


def t_dot(a, b):
    return lax.dot_general(a, b, (((0,), (0,)), ((), ())), preferred_element_type=F32)


def normalize(values):
    wide = values.astype(F32)
    return (wide * lax.rsqrt(jnp.sum(wide * wide, axis=1, keepdims=True) + 1e-06)).astype(BF16)


def kernel(
    student, teacher, target, out,
    raw_s, raw_t, blk, sp, tp, sq, tq, pin, pin2, pzo, po, pacc, tgt, acc, ready, turn, ssem, rsem, lsem,
):
    grp, mem = lax.axis_index("grp"), lax.axis_index("mem")
    z, a = grp // LINE, grp % LINE
    r, x, c = mem // 8, (mem // 2) % NX, mem % 2
    y = r * LINE + a
    way = 1 - 2 * c
    p = a + c * (3 - 2 * a)
    a_meet = 2 - c
    a_of = lambda place: place + c * (3 - 2 * place)
    meet = p == 2
    first_z, last_z = z == 0, z == NZ - 1
    rows = sp.shape[1]

    def at(dz=0, dy=0, dx=0, dc=0):
        yy, zz, xx = (y + dy + NY) % NY, (z + dz + NZ) % NZ, (x + dx) % NX
        cc = (c + dc) % 2
        rank = ((zz * NY + yy) * NX + xx) * 2 + cc
        rank = jnp.where(rank == 0, 2 * NX * NY * NZ, rank)
        return (zz * LINE + yy % LINE, (yy // LINE) * 8 + xx * 2 + cc), rank

    _, my_rank = at()
    two = jnp.where(p == 0, 2, -2) * way
    near = [
        at(dy=way), at(dy=-way), at(dy=two), at(dy=4), at(dz=1), at(dz=-1), at(dx=1), at(dx=3), at(dx=2), at(dc=1),
        at(dz=-1, dy=-way), at(dz=-1, dy=jnp.where(c == 0, way, -2 * way)),
        at(dz=1, dy=jnp.where(p == 1, way, jnp.where(p == 3, -way, 2 * way))),
    ]
    wrap_out = last_z & jnp.logical_not(meet) & (a > 0)
    wrap_in = first_z & jnp.logical_not(meet) & (a > 0)
    forward = meet & jnp.logical_not(last_z)
    used = [p < 3, p > 0, (p == 0) | meet, None, meet | wrap_out, meet | wrap_in] + [None] * 4 + [meet, meet, (p == 1) | (a == 3)]
    earlier = [rank < my_rank for _, rank in near]
    dev = [d for d, _ in near]

    def over(n, cond):
        return cond if used[n] is None else cond & used[n]

    loads = [
        pltpu.make_async_copy(src, dst, lsem.at[k])
        for k, (src, dst) in enumerate(((student, raw_s), (teacher, raw_t), (target, tgt)))
    ]
    for load in loads:
        load.start()
    barrier = pltpu.get_barrier_semaphore()
    for n in range(13):
        @pl.when(over(n, jnp.logical_not(earlier[n])))
        def _():
            pl.semaphore_signal(barrier, 1, device_id=dev[n], device_id_type=MESH)

    me = r * 8 + x * 2 + c
    partner = (1 - r) * 8 + x * 2 + c
    peers = sum(over(n, earlier[n]).astype(jnp.int32) for n in range(13))
    @pl.when(peers > 0)
    def _():
        pl.semaphore_wait(barrier, peers)

    for n in range(13):
        @pl.when(over(n, earlier[n]))
        def _():
            pl.semaphore_signal(ready.at[jnp.where(p == 1, DNEXT, DLAST) if n == UPMEET else BACK[n]], 1, device_id=dev[n], device_id_type=MESH)

    loads[0].wait()
    own = normalize(raw_s[...])
    sp[a] = own
    blk[me] = own

    def wait_ready(n, cond=None):
        here = jnp.logical_not(earlier[n])
        here = over(n, here if cond is None else here & cond)
        @pl.when(here)
        def _():
            pl.semaphore_wait(ready.at[n], 1)

    started = []

    def send(i, src, dst, n, cond=None, end=None):
        copy = pltpu.make_async_remote_copy(
            src_ref=src, dst_ref=dst, send_sem=ssem.at[i], recv_sem=rsem.at[i if end is None else end],
            device_id=dev[n], device_id_type=MESH,
        )
        started.append((copy, cond))
        if cond is None:
            copy.start()
        else:
            pl.when(cond)(copy.start)

    def recv(i, dst, cond=None):
        copy = pltpu.make_async_remote_copy(
            src_ref=dst, dst_ref=dst, send_sem=ssem.at[i], recv_sem=rsem.at[i],
            device_id=dev[RIGHT], device_id_type=MESH,
        )
        if cond is None:
            copy.wait_recv()
        else:
            pl.when(cond)(copy.wait_recv)

    halves = [pl.ds(h * (rows // PARTS), rows // PARTS) for h in range(PARTS)]

    def half_of(whose, h):
        return blk.at[whose] if h is None else blk.at[whose, halves[h]]

    def x_send(base, whose, h=None, cond=None):
        for k, n in enumerate((XUP, XDOWN, XTWO)):
            send(base + k, half_of(whose, h), half_of(whose, h), n, cond)

    def sib_send(i, whose, h=None, cond=None):
        send(i, half_of(whose, h), half_of(whose, h), CORE, cond)

    def x_recv(base, part, sib, h=None, cond=None):
        for k in range(3):
            whose = part * 8 + ((x + NX - HOPS[k]) % NX) * 2 + c
            recv(base + k, half_of(whose, h), cond)
            sib_send(sib + 1 + k, whose, h, cond)

    def xq_recv(cond):
        for h in range(PARTS):
            x_recv(XQ + 3 * h, 1 - r, SIBQ + 4 * h, h, cond)

    def inner(part, whole):
        for k in range(4):
            xx = x if k == 0 else (x + NX - HOPS[k - 1]) % NX
            chip = part * 4 + xx
            if whole:
                recv(SIB + k, blk.at[2 * chip + 1 - c])
            else:
                for h in range(PARTS):
                    recv(SIBQ + 4 * h + k, half_of(2 * chip + 1 - c, h))
            pair = jnp.concatenate([blk[2 * chip], blk[2 * chip + 1]], axis=0)
            cols = pl.ds(pl.multiple_of(chip * 2 * rows, 128), 2 * rows)
            affinity = dot_t(sp[a], pair) - tgt[:, cols]
            acc[...] += jnp.dot(affinity.astype(BF16), pair, preferred_element_type=F32)

    ends = ((p == 3, LEFT, 3), (p == 1, RIGHT, 1), (p == 0, TWO, 0))
    wait_ready(ZUP, meet | wrap_out)
    send(WS, sp.at[a], sq.at[a], ZUP, wrap_out)
    for here, n, place in ends:
        wait_ready(n, here)
        send(SLINE + place, sp.at[a], sp.at[a], n, here)
    send(ZS, sp.at[a], sq.at[a], ZUP, meet)

    def far_send(cond):
        wait_ready(HALF, cond)
        for h in range(PARTS):
            send(FAR + h, half_of(me, h), half_of(me, h), HALF, cond)

    later = jnp.logical_not(first_z)
    loads[1].wait()
    tp[a] = normalize(raw_t[...])
    pieces = [pl.ds(k * (rows // PIECES), rows // PIECES) for k in range(PIECES)]
    for k, piece in enumerate(pieces):
        send(WT + k, tp.at[a, piece], tq.at[a, piece], ZUP, wrap_out)
    for here, n, place in ends[:2]:
        send(TLINE + place, tp.at[a], tp.at[a], n, here)
    ahead, third = len(started) - 1, len(started) - 2
    send(ZT, tp.at[a], tq.at[a], ZUP, meet)
    far_send(first_z)
    wait_ready(CORE)
    sib_send(SIB, me)
    for n in (XUP, XDOWN, XTWO):
        wait_ready(n)
    x_send(XO, me)

    wait_ready(RIGHT, p == 0)
    wait_ready(LEFT, p == 1)

    @pl.when(p == 1)
    def _():
        started[ahead][0].wait_send()
        pl.semaphore_signal(turn, 1, device_id=dev[LEFT], device_id_type=MESH)

    @pl.when(p == 0)
    def _():
        pl.semaphore_wait(turn, 1)

    send(TLINE + 0, tp.at[a], tp.at[a], TWO, p == 0)

    @pl.when(p == 3)
    def _():
        started[third][0].wait_send()

    far_send(later & jnp.logical_not(meet))

    a_next, a_last = 3 - a_meet, 3
    recv(SLINE + 1, sp.at[a_next], meet)
    send(ZS + 1, sp.at[a_next], sq.at[a_next], ZUP, forward)
    recv(TLINE + 1, tp.at[a_next], meet)
    send(ZT + 1, tp.at[a_next], tq.at[a_next], ZUP, forward)
    far_send(later & meet)
    x_recv(XO, r, SIB)
    def take(place, core):
        ap = a_of(place)
        recv(SLINE + place, sp.at[ap], meet)
        send(ZS + 2, sp.at[a_last], sq.at[a_last], ZUP, forward & (c == core))
        recv(TLINE + place, tp.at[ap], meet)
        send(ZT + 2, tp.at[a_last], tq.at[a_last], ZUP, forward & (c == core))

    def join(lo, hi, s_ref, t_ref):
        flat = lambda ref: ref[lo:hi].reshape((hi - lo) * rows, ref.shape[2])
        cross = (dot_t(flat(sp), s_ref[...]) - dot_t(flat(tp), t_ref[...])).astype(BF16)
        theirs = jnp.dot(cross, s_ref[...], preferred_element_type=F32)
        pacc[lo:hi] += theirs.reshape(hi - lo, rows, theirs.shape[1])
        return t_dot(cross, flat(sp))

    def joins(core, *steps):
        @pl.when(meet & (c == core))
        def _():
            for j, lo, hi in steps:
                pacc[j] += join(lo, hi, sp.at[j], tp.at[j])

    take(3, 0)
    pl.when(meet)(lambda: pacc.__setitem__(..., jnp.zeros_like(pacc)))
    joins(0, (2, 1, 2), (3, 1, 3))
    joins(1, (1, 0, 1), (2, 0, 2))
    acc[...] = jnp.zeros_like(acc)
    loads[2].wait()
    inner(r, True)
    take(0, 1)
    joins(0, (0, 1, 4))
    joins(1, (3, 0, 3))

    def give(place, n, cond):
        i = a_of(place)
        pl.when(cond)(lambda: po.__setitem__(i, pacc[i].astype(BF16)))
        send(PF + place, po.at[i], pin, n, cond)

    for n in (LEFT, RIGHT, TWO):
        wait_ready(n, meet)
    give(3, RIGHT, meet & (c == 0))
    give(0, TWO, meet & (c == 1))

    def far_recv(cond):
        for h in range(PARTS):
            recv(FAR + h, half_of(partner, h), cond)
            sib_send(SIBQ + 4 * h, partner, h, cond)
            x_send(XQ + 3 * h, partner, h, cond)

    def across(k, i, places):
        recv(ZS + k, sq.at[i], meet)
        recv(ZT + k, tq.at[i], meet)
        for n in places:
            @pl.when(meet & (i == n))
            def _():
                pzo[n] = join(0, n, sq.at[n], tq.at[n]).astype(BF16)
        send(PZ + k, pzo.at[i], pin2, (ZDOWN, DNEXT, DLAST)[k], meet)

    busy = meet & later
    far_recv(jnp.logical_not(busy))
    xq_recv(meet & first_z)
    for n in (ZDOWN, DNEXT, DLAST):
        wait_ready(n, meet | wrap_in if n == ZDOWN else None)
    across(0, a_meet, (1, 2))
    across(1, a_next, (1, 2))
    far_recv(busy)

    lines = ((3, LEFT, 2), (1, RIGHT, 1), (0, TWO, 2))
    recv(WS, sq.at[a], wrap_in)
    for place, n, k in lines:
        send(ZS + k, sq.at[a], sq.at[a], n, wrap_in & (p == place))
    for q, piece in enumerate(pieces):
        recv(WT + q, tq.at[a, piece], wrap_in)
        for place, n, k in lines:
            send(RT + q, tq.at[a, piece], tq.at[a, piece], n, wrap_in & (p == place), ZT + k)

    xq_recv(jnp.logical_not(meet))
    across(2, a_last, (3,))

    give(0, TWO, meet & (c == 0))
    give(3, RIGHT, meet & (c == 1))
    give(1, LEFT, meet)

    xq_recv(meet & later)
    inner(1 - r, False)

    @pl.when(meet)
    def _():
        acc[...] += pacc[a]

    for place in (0, 1, 3):
        recv(PF + place, pin, p == place)

    @pl.when(jnp.logical_not(meet))
    def _():
        acc[...] += pin[...].astype(F32)

    wait_ready(UPMEET)
    for k, here in enumerate((meet, p == 1, a == 3)):
        recv(PZ + k, pin2, here)

    @pl.when(a > 0)
    def _():
        out[...] = acc[...] + pin2[...].astype(F32)

    @pl.when(a == 0)
    def _():
        out[...] = acc[...]

    for k, (copy, cond) in enumerate(started):
        if k in (ahead, third):
            continue
        if cond is None:
            copy.wait_send()
        else:
            pl.when(cond)(copy.wait_send)


def body(student, teacher, block_target):
    rows, ds = student.shape
    dt = teacher.shape[1]
    columns = block_target.shape[1]
    weight = 16.0 * math.sqrt(ds / columns)
    vmem = pl.BlockSpec(memory_space=pltpu.VMEM)
    part = pl.pallas_call(
        kernel,
        out_shape=jax.ShapeDtypeStruct((rows, ds), F32),
        in_specs=[pl.BlockSpec(memory_space=pltpu.HBM)] * 3,
        out_specs=vmem,
        scratch_shapes=[
            pltpu.VMEM((rows, ds), BF16),
            pltpu.VMEM((rows, dt), BF16),
            pltpu.VMEM((16, rows, ds), BF16),
            pltpu.VMEM((4, rows, ds), BF16),
            pltpu.VMEM((4, rows, dt), BF16),
            pltpu.VMEM((4, rows, ds), BF16),
            pltpu.VMEM((4, rows, dt), BF16),
            pltpu.VMEM((rows, ds), BF16),
            pltpu.VMEM((rows, ds), BF16),
            pltpu.VMEM((4, rows, ds), BF16),
            pltpu.VMEM((4, rows, ds), BF16),
            pltpu.VMEM((4, rows, ds), F32),
            pltpu.VMEM((rows, columns), F32),
            pltpu.VMEM((rows, ds), F32),
            pltpu.SemaphoreType.REGULAR((13,)),
            pltpu.SemaphoreType.REGULAR,
            pltpu.SemaphoreType.DMA((COPIES,)),
            pltpu.SemaphoreType.DMA((COPIES,)),
            pltpu.SemaphoreType.DMA((3,)),
        ],
        compiler_params=pltpu.CompilerParams(
            collective_id=0, has_side_effects=True, vmem_limit_bytes=62 * 2**20
        ),
    )(student, teacher, block_target)
    return part * weight


def solution(mesh):
    spec = P(("grp", "mem"), None)
    return jax.shard_map(body, mesh=mesh, in_specs=(spec,) * 3, out_specs=spec, check_vma=False)
```

time: 65 us -> 59.6 us (0.917)
  local copies, waits for them, and re-layouts: 3.62 us -> 0 us
  Pallas kernels: 60.2 us -> 57.7 us
  other arithmetic: 0.78 us -> 1.78 us
    unnamed x6 -> x0, local copies, waits for them, and re-layouts: 3.62 us -> none
    pallas_call x1, Pallas kernels: 60.2 us -> 57.7 us  [body(): pl.pallas_call(kernel, out_shape=jax.ShapeDtypeStruct((rows, ds), F32), i...]
    mul x1, other arithmetic: 0.78 us -> 1.78 us  [body(): return part * weight]
where the time goes in v2:
time: 59.6 us; the launch traced here: 59.4 us
  Pallas kernels  57.7 us (97%)
  other arithmetic  1.78 us (3%)
    pallas_call x1, Pallas kernels, body(): pl.pallas_call(kernel, out_shape=jax.ShapeDtypeStruct((rows, ds), F32), i...  57.7 us
    mul x1, other arithmetic, body(): return part * weight  1.78 us

profile of v2, /device:TPU:1, one launch (start us, length us, event | category | flops | bytes accessed | tf_op | source)
XLA Modules:
  0.0 59.4 jit_solution(12584956665638487662)
XLA Ops:
  0.0 57.7 %shard_map.37 = f32[192,512]{1,0:T(8,128)} custom-call(bf16[192,512]{1,0:T(8,128)(2,1)} %student.1, bf16[192,1280]{1,0:T(8,128)(2,1)} %teacher.1, f32[192,3072]{1,0:T(8,128)} %target.1), custom_call_target="tpu_custom_call" | custom-call | tf_op jit(solution)/shard_map/pallas_call | solution.py:352
  57.7 1.8 %broadcast_multiply_fusion = f32[192,512]{1,0:T(8,128)} fusion(f32[192,512]{1,0:T(8,128)} %shard_map.37), kind=kLoop, calls=%fused_computation | loop fusion | flops 98304 | bytes 786432 | tf_op jit(solution)/shard_map/mul | solution.py:382

commit v3 on v2

--- a/solution.py
+++ b/solution.py
@@ -193,7 +193,8 @@
         send(TLINE + place, tp.at[a], tp.at[a], n, here)
     ahead, third = len(started) - 1, len(started) - 2
     send(ZT, tp.at[a], tq.at[a], ZUP, meet)
-    far_send(first_z)
+    early = first_z & (a == 0)
+    far_send(early)
     wait_ready(CORE)
     sib_send(SIB, me)
     for n in (XUP, XDOWN, XTWO):
@@ -218,14 +219,14 @@
     def _():
         started[third][0].wait_send()
 
-    far_send(later & jnp.logical_not(meet))
+    far_send(jnp.logical_not(early | meet))
 
     a_next, a_last = 3 - a_meet, 3
     recv(SLINE + 1, sp.at[a_next], meet)
     send(ZS + 1, sp.at[a_next], sq.at[a_next], ZUP, forward)
     recv(TLINE + 1, tp.at[a_next], meet)
     send(ZT + 1, tp.at[a_next], tq.at[a_next], ZUP, forward)
-    far_send(later & meet)
+    far_send(meet)
     x_recv(XO, r, SIB)
     def take(place, core):
         ap = a_of(place)

time: 59.6 us -> 59.8 us (level); the launches traced: 59.4 us -> 58.9 us
  Pallas kernels: 57.7 us -> 57.1 us
where the time goes in v3:
time: 59.8 us; the launch traced here: 58.9 us
  Pallas kernels  57.1 us (95%)
  other arithmetic  1.78 us (3%)
    pallas_call x1, Pallas kernels, body(): pl.pallas_call(kernel, out_shape=jax.ShapeDtypeStruct((rows, ds), F32), i...  57.1 us
    mul x1, other arithmetic, body(): return part * weight  1.78 us

profile of v3, /device:TPU:1, one launch (start us, length us, event | category | flops | bytes accessed | tf_op | source)
XLA Modules:
  0.0 58.9 jit_solution(2971393976557769884)
XLA Ops:
  0.0 57.1 %shard_map.37 = f32[192,512]{1,0:T(8,128)} custom-call(bf16[192,512]{1,0:T(8,128)(2,1)} %student.1, bf16[192,1280]{1,0:T(8,128)(2,1)} %teacher.1, f32[192,3072]{1,0:T(8,128)} %target.1), custom_call_target="tpu_custom_call" | custom-call | tf_op jit(solution)/shard_map/pallas_call | solution.py:353
  57.1 1.8 %broadcast_multiply_fusion = f32[192,512]{1,0:T(8,128)} fusion(f32[192,512]{1,0:T(8,128)} %shard_map.37), kind=kLoop, calls=%fused_computation | loop fusion | flops 98304 | bytes 786432 | tf_op jit(solution)/shard_map/mul | solution.py:383
